TPU v7x, 32 devices: a whole 2x2x4 slice. The times are simulated.
32 devices in a mesh: leaf: 16 (over z, y, x), cone: 2 (over core).
Axes of the slice: x: 2, y: 2, z: 4, core: 2. Of those that a mesh axis runs over, the one named last changes fastest.
Arguments:
- coefficients: bfloat16 [128, 4, 3, 32, 256], P('leaf', 'cone'), may hold values from -6 to 6
- local_to_target: bfloat16 [128, 4, 256, 768], P('leaf', 'cone'), may hold values from -0.1875 to 0.1875
- send_map: int32 [16, 16, 32], P('leaf'), may hold values from -1 to 255, as said below
- test_weight: bfloat16 [16, 16, 32, 108], P('leaf'), may hold values from -1 to 1
- slot_edge: int32 [3, 16, 16, 32], P(None, 'leaf'), may hold values from -1 to 383, as said below
- shared_edges: int32 [16, 2, 32], P('leaf'), may hold values from 0 to 383, as said below
Outputs:
- tested: float32 [2, 32, 6144], P(None, 'cone', 'leaf')
Inputs may be any that keep to these rules, and one draw needn't show every extreme that they name: Each of the 256 triangles of a leaf device s stands in exactly one slot of send_map[s]; every other slot is -1. In every draw, each leaf device fills all 32 slots of its block to some owner. slot_edge[e, d, s, n] is -1 exactly where send_map[s, d, n] is -1. The 64 numbers of shared_edges[d] are distinct.
All inputs are finite; a program needn't handle non-finite values.
Results may differ from a plain program's by a relative error of at most 0.0029.
Values may be sent and summed in bfloat16 or wider, within the bound.
A program may use at most 64 MiB of HBM per device.

v0:
```python
import jax
import jax.numpy as jnp
from jax import lax
from jax.sharding import PartitionSpec as P

QUAD = 12
TRI_LEAF = 32
EDGE_DEV = 384


def extended(array, sides, width):
    for axis, dim in sides:
        peers, length = (lax.axis_size(axis), array.shape[dim])
        up = [(i, (i + 1) % peers) for i in range(peers - 1)]
        down = [(j, i) for i, j in up]
        last = lax.slice_in_dim(array, length - width, length, axis=dim)
        leading = lax.slice_in_dim(array, 0, width, axis=dim)
        before = lax.ppermute(last, axis, up)
        after = lax.ppermute(leading, axis, down)
        array = jnp.concatenate([before, array, after], axis=dim)
    return array


def tested_slots(weights, fields, rhs_count, result_form):
    peer_count, capacity = (weights.shape[0], weights.shape[1])
    weight_view = weights.reshape(peer_count, capacity, 3, QUAD, 3)
    field_view = fields.reshape(peer_count, capacity, QUAD, 2, 3, rhs_count)
    return jnp.einsum(
        "scepk,scpikh->" + result_form, weight_view, field_view, preferred_element_type=jnp.float32
    )


def body(coefficients, local_to_target, send_map, test_weight, slot_edge, shared_edges):
    partial_field = jnp.einsum(
        "lkchr,lkrq->lqch", coefficients, local_to_target, preferred_element_type=jnp.float32
    )
    cone_count = lax.axis_size("cone")
    rhs_count = partial_field.shape[3] // cone_count
    summed = lax.psum(partial_field, "cone")
    rhs_share = lax.dynamic_slice_in_dim(summed, lax.axis_index("cone") * rhs_count, rhs_count, 3)
    rhs_share = rhs_share.astype(jnp.bfloat16)
    leaf_count = rhs_share.shape[0]
    tri_rows = rhs_share.reshape(leaf_count * TRI_LEAF, -1)
    send_rows = send_map[0]
    is_live = send_rows >= 0
    safe_rows = jnp.where(is_live, send_rows, 0)
    picked = tri_rows[safe_rows]
    outgoing = jnp.where(is_live[:, :, None], picked, jnp.zeros((), jnp.bfloat16))
    weights = test_weight[0]
    arrived = lax.all_to_all(outgoing, "leaf", split_axis=0, concat_axis=0, tiled=True)
    partial_value = tested_slots(weights, arrived, rhs_count, "escih")
    edge_ids = slot_edge[:, 0].reshape(-1)
    values = partial_value.reshape(-1, 2 * rhs_count)
    onehot = (edge_ids[:, None] == jnp.arange(EDGE_DEV, dtype=jnp.int32)[None, :]).astype(
        jnp.float32
    )
    edge_sum = jnp.einsum(
        "ra,re->ae",
        values,
        onehot,
        precision=lax.Precision.HIGHEST,
        preferred_element_type=jnp.float32,
    )
    lower_ids = shared_edges[0, 0]
    upper_ids = shared_edges[0, 1]
    share_width = lower_ids.shape[0]
    rim_values = jnp.concatenate([edge_sum[:, lower_ids], edge_sum[:, upper_ids]], axis=1)
    padded = extended(rim_values, (("leaf", 1),), share_width)
    total = (
        edge_sum.at[:, lower_ids]
        .add(padded[:, :share_width])
        .at[:, upper_ids]
        .add(padded[:, 3 * share_width :])
    )
    return total.reshape(2, rhs_count, -1)


def solution(mesh):
    placed = (
        P("leaf", "cone", None, None, None),
        P("leaf", "cone", None, None),
        P("leaf", None, None),
        P("leaf", None, None, None),
        P(None, "leaf", None, None),
        P("leaf", None, None),
    )
    return jax.shard_map(
        body, mesh=mesh, in_specs=placed, out_specs=P(None, "cone", "leaf"), check_vma=False
    )
```

profile of v0, /device:TPU:6, one launch (start us, length us, event | category | flops | bytes accessed | tf_op | source)
XLA Modules:
  0.0 120.5 jit_solution(16568541062340450514)
XLA Ops:
  0.0 0.0 copy-start
  0.0 0.8 compare_select_fusion
  0.8 0.7 compare_bitcast_fusion
  1.5 5.3 %fusion.3 = f32[8,768,3,32]{1,3,2,0:T(8,128)} fusion(bf16[8,2,3,32,256]{4,3,2,1,0:T(8,128)(2,1)S(1)} %copy-done, bf16[8,2,256,768]{3,2,1,0:T(8,128)(2,1)} %param.7), kind=kOutput, calls=%fused_computation.9 | convolution fusion | flops 603979776 | bytes 9437184 | tf_op jit(solution)/shard_map/lkchr,lkrq->lqch/dot_general | solution.py:34
  6.8 10.3 %all-reduce.1 = bf16[8,768,3,32]{1,3,2,0:T(8,128)(2,1)S(1)} all-reduce(f32[8,768,3,32]{1,3,2,0:T(8,128)} %fusion.3), channel_id=1, replica_groups=mesh['leaf'=16,'cone'=2] {'cone'}, use_global_device_ids=true, to_apply=%region_0.0 | all-reduce | flops 589824 | bytes 3538944 | tf_op jit(solution)/shard_map/psum | solution.py:39
  17.1 6.7 %copy.25 = bf16[8,768,3,16]{3,2,1,0:T(4,128)(2,1)} copy(bf16[8,768,3,16]{1,3,2,0:T(8,128)(2,1)S(1)} %dynamic-slice_convert_fusion) | data formatting | bytes 1179648 | tf_op jit(solution)/shard_map/convert_element_type | solution.py:41
  23.9 9.3 %reshape.102 = bf16[256,1152]{1,0:T(8,128)(2,1)S(1)} reshape(bf16[8,768,3,16]{3,2,1,0:T(4,128)(2,1)} %copy.25) | data formatting | bytes 1179648 | tf_op jit(solution)/shard_map/reshape | solution.py:43
  33.2 0.1 reshape.108
  33.3 2.1 %gather_fusion = bf16[512,1152]{1,0:T(8,128)(2,1)S(1)} fusion(bf16[256,1152]{1,0:T(8,128)(2,1)S(1)} %reshape.102, s32[1024]{0:T(1024)S(1)} %pad_clamp_fusion.2), kind=kCustom, calls=%fused_computation | custom fusion | bytes 2361344 | tf_op jit(solution)/shard_map/gather | solution.py:47
  35.4 0.0 copy-start.2
  35.4 1.2 %broadcast_select_fusion = bf16[16,32,1152]{2,1,0:T(8,128)(2,1)} fusion(bf16[16,32,1152]{2,1,0:T(8,128)(2,1)S(1)} %bitcast.58, pred[16,32]{1,0:T(8,128)(4,1)S(1)} %compare_bitcast_fusion), kind=kLoop, calls=%fused_computation.13 | loop fusion | flops 589824 | bytes 2359808 | tf_op jit(solution)/shard_map/jit(_where)/select_n | solution.py:48
  36.6 7.4 %all-to-all-start = ((bf16[16,32,1152]{2,1,0:T(8,128)(2,1)}), bf16[16,32,1152]{2,1,0:T(8,128)(2,1)S(1)}, u32[]{:S(2)}, u32[]{:S(2)}) async-start(bf16[16,32,1152]{2,1,0:T(8,128)(2,1)} %broadcast_select_fusion), calls=%async_computation | async-start | bytes 2359296 | tf_op jit(solution)/shard_map/all_to_all | solution.py:50
  44.0 0.4 copy.27
  44.4 2.5 %copy.37 = bf16[16,32,3,12,3,1]{3,2,4,5,1,0:T(4,128)(2,1)} copy(bf16[16,32,3,12,3,1]{1,0,4,3,2,5:T(8,128)(2,1)S(1)} %bitcast.59) | data formatting | bytes 221184 | tf_op jit(solution)/shard_map/reshape;squeeze | solution.py:26
  47.0 0.1 eq.15
  47.1 23.8 %all-to-all-done = bf16[16,32,1152]{2,1,0:T(8,128)(2,1)S(1)} async-done(((bf16[16,32,1152]{2,1,0:T(8,128)(2,1)}), bf16[16,32,1152]{2,1,0:T(8,128)(2,1)S(1)}, u32[]{:S(2)}, u32[]{:S(2)}) %all-to-all-start) | async-done | bytes 1179680 | tf_op jit(solution)/shard_map/all_to_all | solution.py:50
  70.9 3.3 %copy.26 = bf16[16,32,1152]{1,2,0:T(8,128)(2,1)} copy(bf16[16,32,1152]{2,1,0:T(8,128)(2,1)S(1)} %all-to-all-done) | data formatting | bytes 2359296 | tf_op jit(solution)/shard_map/all_to_all | solution.py:50
  74.2 19.7 %copy.28 = bf16[16,32,12,2,3,16]{5,2,4,3,1,0:T(8,128)(2,1)} copy(bf16[16,32,12,2,3,16]{1,5,4,3,2,0:T(8,128)(2,1)} %bitcast.57) | data formatting | bytes 2359296 | tf_op jit(solution)/shard_map/reshape | solution.py:27
  93.9 0.0 copy-done.1
  93.9 6.6 %convolution_bitcast_fusion = f32[3,16,32,2,16]{4,0,3,2,1:T(4,128)} fusion(bf16[16,32,12,2,3,16]{5,2,4,3,1,0:T(8,128)(2,1)} %copy.28, bf16[16,32,3,12,3,1]{3,2,4,5,1,0:T(4,128)(2,1)S(1)} %copy-done.1), kind=kOutput, calls=%fused_computation.10 | convolution fusion | flops 3538944 | bytes 1486848 | tf_op jit(solution)/shard_map/scepk,scpikh->escih/dot_general | solution.py:28
  100.5 1.8 %copy.30 = f32[3,16,32,2,16]{2,1,0,4,3:T(8,128)S(1)} copy(f32[3,16,32,2,16]{4,0,3,2,1:T(4,128)} %convolution_bitcast_fusion) | data formatting | bytes 393216 | tf_op jit(solution)/shard_map/scepk,scpikh->escih/transpose | solution.py:28
  102.4 0.3 reshape.104
  102.7 2.2 %fusion.2 = f32[32,384]{0,1:T(8,128)S(1)} fusion(f32[1536,32]{0,1:T(8,128)S(1)} %reshape.104, s32[1536]{0:T(1024)S(1)} %eq.15), kind=kOutput, calls=%fused_computation.8 | convolution fusion | flops 227082240 | bytes 251904 | tf_op jit(solution)/shard_map/ra,re->ae/dot_general | solution.py:57
  104.9 0.6 gather_fusion.1
  105.5 5.4 %collective-permute-start = (f32[32,32]{0,1:T(8,128)S(1)}, f32[32,32]{0,1:T(8,128)S(1)}, u32[]{:S(2)}, u32[]{:S(2)}) collective-permute-start(f32[32,32]{0,1:T(8,128)S(1)} %bitcast.61), channel_id=1, source_target_pairs={{0,2},{2,4},{4,6},{6,8},{8,10},{10,12},{12,14},{14,16},{16,18},{18... | collective-permute-start | bytes 12296 | tf_op jit(solution)/shard_map/ppermute | solution.py:18
  111.0 0.6 gather_fusion.2
  111.5 1.9 %collective-permute-start.1 = (f32[32,32]{0,1:T(8,128)S(1)}, f32[32,32]{0,1:T(8,128)S(1)}, u32[]{:S(2)}, u32[]{:S(2)}) collective-permute-start(f32[32,32]{0,1:T(8,128)S(1)} %bitcast.60), channel_id=1, source_target_pairs={{2,0},{4,2},{6,4},{8,6},{10,8},{12,10},{14,12},{16,14},{18,16},{20... | collective-permute-start | bytes 12296 | tf_op jit(solution)/shard_map/ppermute | solution.py:19
  113.5 0.0 collective-permute-done
  113.5 0.8 scatter_custom_fusion
  114.3 4.6 %collective-permute-done.1 = f32[32,32]{0,1:T(8,128)S(1)} collective-permute-done((f32[32,32]{0,1:T(8,128)S(1)}, f32[32,32]{0,1:T(8,128)S(1)}, u32[]{:S(2)}, u32[]{:S(2)}) %collective-permute-start.1) | collective-permute-done | bytes 4128 | tf_op jit(solution)/shard_map/ppermute | solution.py:19
  119.0 0.8 scatter_custom_fusion.1
  119.8 0.7 copy.34
  (11 shorter events, 0.1 us)
Async XLA Ops:
  0.0 1.5 %copy-start = (bf16[8,2,3,32,256]{4,3,2,1,0:T(8,128)(2,1)S(1)}, bf16[8,2,3,32,256]{4,3,2,1,0:T(8,128)(2,1)}, u32[]{:S(2)}) copy-start(bf16[8,2,3,32,256]{4,3,2,1,0:T(8,128)(2,1)} %param.6) | copy-start | bytes 2359300
  35.4 8.6 %copy-start.2 = (bf16[1,16,32,108]{3,2,1,0:T(8,128)(2,1)S(1)}, bf16[1,16,32,108]{3,2,1,0:T(8,128)(2,1)}, u32[]{:S(2)}) copy-start(bf16[1,16,32,108]{3,2,1,0:T(8,128)(2,1)} %param.9) | copy-start | bytes 331780
  36.6 10.3 %copy-start.3 = (s32[3,1,16,32]{3,2,1,0:T(8,128)S(1)}, s32[3,1,16,32]{3,2,1,0:T(8,128)}, u32[]{:S(2)}) copy-start(s32[3,1,16,32]{3,2,1,0:T(8,128)} %param.10) | copy-start | bytes 18436
  36.6 10.4 %copy-start.4 = (s32[1,2,32]{2,1,0:T(2,128)S(1)}, s32[1,2,32]{2,1,0:T(2,128)}, u32[]{:S(2)}) copy-start(s32[1,2,32]{2,1,0:T(2,128)} %param.11) | copy-start | bytes 772
  36.6 34.2 %all-to-all-start = ((bf16[16,32,1152]{2,1,0:T(8,128)(2,1)}), bf16[16,32,1152]{2,1,0:T(8,128)(2,1)S(1)}, u32[]{:S(2)}, u32[]{:S(2)}) async-start(bf16[16,32,1152]{2,1,0:T(8,128)(2,1)} %broadcast_select_fusion), calls=%async_computation | async-start | bytes 2359296 | tf_op jit(solution)/shard_map/all_to_all | solution.py:50
  74.2 19.7 %copy-start.1 = (bf16[16,32,3,12,3,1]{3,2,4,5,1,0:T(4,128)(2,1)S(1)}, bf16[16,32,3,12,3,1]{3,2,4,5,1,0:T(4,128)(2,1)}, u32[]{:S(2)}) copy-start(bf16[16,32,3,12,3,1]{3,2,4,5,1,0:T(4,128)(2,1)} %copy.37) | copy-start | bytes 331780
  105.5 7.9 %collective-permute-start = (f32[32,32]{0,1:T(8,128)S(1)}, f32[32,32]{0,1:T(8,128)S(1)}, u32[]{:S(2)}, u32[]{:S(2)}) collective-permute-start(f32[32,32]{0,1:T(8,128)S(1)} %bitcast.61), channel_id=1, source_target_pairs={{0,2},{2,4},{4,6},{6,8},{8,10},{10,12},{12,14},{14,16},{16,18},{18... | collective-permute-start | bytes 12296 | tf_op jit(solution)/shard_map/ppermute | solution.py:18
  111.5 7.4 %collective-permute-start.1 = (f32[32,32]{0,1:T(8,128)S(1)}, f32[32,32]{0,1:T(8,128)S(1)}, u32[]{:S(2)}, u32[]{:S(2)}) collective-permute-start(f32[32,32]{0,1:T(8,128)S(1)} %bitcast.60), channel_id=1, source_target_pairs={{2,0},{4,2},{6,4},{8,6},{10,8},{12,10},{14,12},{16,14},{18,16},{20... | collective-permute-start | bytes 12296 | tf_op jit(solution)/shard_map/ppermute | solution.py:19
where the time goes:
time: 121 us
  local copies, waits for them, and re-layouts  48.4 us (40%)
  waiting for transfers between devices  28.4 us (23%)
  starting transfers between devices  14.7 us (12%)
  matrix products  14.2 us (12%)
  blocking collectives  10.3 us (9%)
  other arithmetic  4.39 us (4%)
    all_to_all x1, waiting for transfers between devices, body(): lax.all_to_all(outgoing, 'leaf', split_axis=0, concat_axis=0, tiled=True)  23.8 us
    reshape x1, local copies, waits for them, and re-layouts, tested_slots(): field_view = fields.reshape(peer_count, capacity, QUAD, 2, 3, rhs_count)  19.7 us
    psum x1, blocking collectives, body(): summed = lax.psum(partial_field, 'cone')  10.3 us
    reshape x1, local copies, waits for them, and re-layouts, body(): tri_rows = rhs_share.reshape(leaf_count * TRI_LEAF, -1)  9.31 us
    all_to_all x1, starting transfers between devices, body(): lax.all_to_all(outgoing, 'leaf', split_axis=0, concat_axis=0, tiled=True)  7.4 us
    convert_element_type x2, local copies, waits for them, and re-layouts, body(): rhs_share = rhs_share.astype(jnp.bfloat16)  6.78 us
    dot_general x1, matrix products, tested_slots(): jnp.einsum('scepk,scpikh->' + result_form, weight_view, field_view, prefe...  6.63 us
    ppermute x1, starting transfers between devices, extended(): before = lax.ppermute(last, axis, up)  5.42 us
  transfers between devices with their start and end apart: 3, of which 2 were waited for; matrix products, arithmetic and copies ran while one was open for 4% of the time, Pallas kernels for 0%

commit v1 on v0

--- a/solution.py
+++ b/solution.py
@@ -36,7 +36,7 @@
     )
     cone_count = lax.axis_size("cone")
     rhs_count = partial_field.shape[3] // cone_count
-    summed = lax.psum(partial_field, "cone")
+    summed = jnp.sum(lax.all_gather(partial_field, "cone"), axis=0)
     rhs_share = lax.dynamic_slice_in_dim(summed, lax.axis_index("cone") * rhs_count, rhs_count, 3)
     rhs_share = rhs_share.astype(jnp.bfloat16)
     leaf_count = rhs_share.shape[0]

time: 121 us -> 142 us (1.17)
  waiting for transfers between devices: 28.4 us -> 43.7 us
  between operations: 0.12 us -> 13.5 us
  blocking collectives: 10.3 us -> 0 us
  local copies, waits for them, and re-layouts: 48.4 us -> 50.1 us
    all_gather x0 -> x1, waiting for transfers between devices: none -> 15.3 us  [body(): summed = jnp.sum(lax.all_gather(partial_field, 'cone'), axis=0)]
    psum x1 -> x0, blocking collectives: 10.3 us -> none  [body(): summed = lax.psum(partial_field, 'cone')]
    reduce_sum x0 -> x1, other arithmetic: none -> 2.85 us  [body(): summed = jnp.sum(lax.all_gather(partial_field, 'cone'), axis=0)]
    unnamed x11 -> x13, local copies, waits for them, and re-layouts: 0.41 us -> 2.21 us
  transfers between devices with their start and end apart: 3 -> 4, of which waited for: 2 -> 3; matrix products, arithmetic and copies ran while one was open for 4% -> 3% of each run, Pallas kernels for 0% -> 0%
where the time goes in v1:
time: 142 us
  local copies, waits for them, and re-layouts  50.1 us (35%)
  waiting for transfers between devices  43.7 us (31%)
  starting transfers between devices  14.4 us (10%)
  matrix products  14.2 us (10%)
  between operations  13.5 us (10%)
  other arithmetic  5.78 us (4%)
    all_to_all x1, waiting for transfers between devices, body(): lax.all_to_all(outgoing, 'leaf', split_axis=0, concat_axis=0, tiled=True)  23.7 us
    reshape x1, local copies, waits for them, and re-layouts, tested_slots(): field_view = fields.reshape(peer_count, capacity, QUAD, 2, 3, rhs_count)  19.6 us
    all_gather x1, waiting for transfers between devices, body(): summed = jnp.sum(lax.all_gather(partial_field, 'cone'), axis=0)  15.3 us
    reshape x1, local copies, waits for them, and re-layouts, body(): tri_rows = rhs_share.reshape(leaf_count * TRI_LEAF, -1)  9.31 us
    all_to_all x1, starting transfers between devices, body(): lax.all_to_all(outgoing, 'leaf', split_axis=0, concat_axis=0, tiled=True)  7.11 us
    convert_element_type x2, local copies, waits for them, and re-layouts, body(): rhs_share = rhs_share.astype(jnp.bfloat16)  6.76 us
    dot_general x1, matrix products, tested_slots(): jnp.einsum('scepk,scpikh->' + result_form, weight_view, field_view, prefe...  6.63 us
    ppermute x1, starting transfers between devices, extended(): before = lax.ppermute(last, axis, up)  5.4 us
  transfers between devices with their start and end apart: 4, of which 3 were waited for; matrix products, arithmetic and copies ran while one was open for 3% of the time, Pallas kernels for 0%

profile of v1, /device:TPU:6, one launch (start us, length us, event | category | flops | bytes accessed | tf_op | source)
XLA Modules:
  0.0 141.7 jit_solution(10444902585395165806)
XLA Ops:
  6.5 1.1 copy-done
  7.7 5.3 %fusion.3 = f32[8,768,3,32]{1,3,2,0:T(8,128)} fusion(bf16[8,2,3,32,256]{4,3,2,1,0:T(8,128)(2,1)S(1)} %copy-done, bf16[8,2,256,768]{3,2,1,0:T(8,128)(2,1)} %param.7), kind=kOutput, calls=%fused_computation.9 | convolution fusion | flops 603979776 | bytes 9437184 | tf_op jit(solution)/shard_map/lkchr,lkrq->lqch/dot_general | solution.py:34
  13.0 0.0 all-gather.3.cloned.1.call-update
  13.0 0.7 copy-done.3
  13.7 0.1 reshape.108
  13.8 15.3 %all-gather.3.cloned.1.call-done = f32[16,768,3,32]{1,3,2,0:T(8,128)} async-done(((f32[8,768,3,32]{1,3,2,0:T(8,128)}), f32[16,768,3,32]{1,3,2,0:T(8,128)}) %all-gather.3.cloned.1.call-update) | async-done | bytes 4718608 | tf_op jit(solution)/shard_map/all_gather | solution.py:39
  29.1 2.8 %reduce_sum.9 = bf16[8,768,3,32]{1,3,2,0:T(8,128)(2,1)S(1)} reduce(f32[2,8,768,3,32]{2,4,3,1,0:T(8,128)} %bitcast.60, f32[]{:T(128)} %constant.9.clone.1), dimensions={0}, to_apply=%region_0.0 | reduce | flops 589824 | bytes 5898244 | tf_op jit(solution)/shard_map/reduce_sum | solution.py:39
  32.0 6.7 %copy.24 = bf16[8,768,3,16]{3,2,1,0:T(4,128)(2,1)} copy(bf16[8,768,3,16]{1,3,2,0:T(8,128)(2,1)S(1)} %dynamic-slice_convert_fusion) | data formatting | bytes 1179648 | tf_op jit(solution)/shard_map/convert_element_type | solution.py:41
  38.7 9.3 %reshape.102 = bf16[256,1152]{1,0:T(8,128)(2,1)S(1)} reshape(bf16[8,768,3,16]{3,2,1,0:T(4,128)(2,1)} %copy.24) | data formatting | bytes 1179648 | tf_op jit(solution)/shard_map/reshape | solution.py:43
  48.0 2.1 %gather_fusion = bf16[512,1152]{1,0:T(8,128)(2,1)S(1)} fusion(bf16[256,1152]{1,0:T(8,128)(2,1)S(1)} %reshape.102, s32[1024]{0:T(1024)S(1)} %pad_clamp_fusion.2), kind=kCustom, calls=%fused_computation | custom fusion | bytes 2361344 | tf_op jit(solution)/shard_map/gather | solution.py:47
  50.1 0.0 copy-start.2
  50.2 1.2 broadcast_select_fusion
  51.4 7.1 %all-to-all-start = ((bf16[16,32,1152]{2,1,0:T(8,128)(2,1)}), bf16[16,32,1152]{2,1,0:T(8,128)(2,1)S(1)}, u32[]{:S(2)}, u32[]{:S(2)}) async-start(bf16[16,32,1152]{2,1,0:T(8,128)(2,1)} %broadcast_select_fusion), calls=%async_computation | async-start | bytes 2359296 | tf_op jit(solution)/shard_map/all_to_all | solution.py:50
  58.5 0.4 copy.26
  58.9 2.5 %copy.36 = bf16[16,32,3,12,3,1]{3,2,4,5,1,0:T(4,128)(2,1)} copy(bf16[16,32,3,12,3,1]{1,0,4,3,2,5:T(8,128)(2,1)S(1)} %bitcast.61) | data formatting | bytes 221184 | tf_op jit(solution)/shard_map/reshape;squeeze | solution.py:26
  61.4 0.1 eq.15
  61.5 23.7 %all-to-all-done = bf16[16,32,1152]{2,1,0:T(8,128)(2,1)S(1)} async-done(((bf16[16,32,1152]{2,1,0:T(8,128)(2,1)}), bf16[16,32,1152]{2,1,0:T(8,128)(2,1)S(1)}, u32[]{:S(2)}, u32[]{:S(2)}) %all-to-all-start) | async-done | bytes 1179680 | tf_op jit(solution)/shard_map/all_to_all | solution.py:50
  85.3 3.3 %copy.25 = bf16[16,32,1152]{1,2,0:T(8,128)(2,1)} copy(bf16[16,32,1152]{2,1,0:T(8,128)(2,1)S(1)} %all-to-all-done) | data formatting | bytes 2359296 | tf_op jit(solution)/shard_map/all_to_all | solution.py:50
  88.6 19.6 %copy.27 = bf16[16,32,12,2,3,16]{5,2,4,3,1,0:T(8,128)(2,1)} copy(bf16[16,32,12,2,3,16]{1,5,4,3,2,0:T(8,128)(2,1)} %bitcast.58) | data formatting | bytes 2359296 | tf_op jit(solution)/shard_map/reshape | solution.py:27
  108.3 6.6 %convolution_bitcast_fusion = f32[3,16,32,2,16]{4,0,3,2,1:T(4,128)} fusion(bf16[16,32,12,2,3,16]{5,2,4,3,1,0:T(8,128)(2,1)} %copy.27, bf16[16,32,3,12,3,1]{3,2,4,5,1,0:T(4,128)(2,1)S(1)} %copy-done.1), kind=kOutput, calls=%fused_computation.10 | convolution fusion | flops 3538944 | bytes 1486848 | tf_op jit(solution)/shard_map/scepk,scpikh->escih/dot_general | solution.py:28
  114.9 1.8 %copy.29 = f32[3,16,32,2,16]{2,1,0,4,3:T(8,128)S(1)} copy(f32[3,16,32,2,16]{4,0,3,2,1:T(4,128)} %convolution_bitcast_fusion) | data formatting | bytes 393216 | tf_op jit(solution)/shard_map/scepk,scpikh->escih/transpose | solution.py:28
  116.8 0.3 reshape.104
  117.1 2.2 %fusion.2 = f32[32,384]{0,1:T(8,128)S(1)} fusion(f32[1536,32]{0,1:T(8,128)S(1)} %reshape.104, s32[1536]{0:T(1024)S(1)} %eq.15), kind=kOutput, calls=%fused_computation.8 | convolution fusion | flops 227082240 | bytes 251904 | tf_op jit(solution)/shard_map/ra,re->ae/dot_general | solution.py:57
  119.3 0.6 gather_fusion.1
  119.9 5.4 %collective-permute-start = (f32[32,32]{0,1:T(8,128)S(1)}, f32[32,32]{0,1:T(8,128)S(1)}, u32[]{:S(2)}, u32[]{:S(2)}) collective-permute-start(f32[32,32]{0,1:T(8,128)S(1)} %bitcast.63), channel_id=1, source_target_pairs={{0,2},{2,4},{4,6},{6,8},{8,10},{10,12},{12,14},{14,16},{16,18},{18... | collective-permute-start | bytes 12296 | tf_op jit(solution)/shard_map/ppermute | solution.py:18
  125.3 0.6 gather_fusion.2
  125.9 1.9 %collective-permute-start.1 = (f32[32,32]{0,1:T(8,128)S(1)}, f32[32,32]{0,1:T(8,128)S(1)}, u32[]{:S(2)}, u32[]{:S(2)}) collective-permute-start(f32[32,32]{0,1:T(8,128)S(1)} %bitcast.62), channel_id=1, source_target_pairs={{2,0},{4,2},{6,4},{8,6},{10,8},{12,10},{14,12},{16,14},{18,16},{20... | collective-permute-start | bytes 12296 | tf_op jit(solution)/shard_map/ppermute | solution.py:19
  127.8 0.0 collective-permute-done
  127.8 0.8 scatter_custom_fusion
  128.7 4.6 %collective-permute-done.1 = f32[32,32]{0,1:T(8,128)S(1)} collective-permute-done((f32[32,32]{0,1:T(8,128)S(1)}, f32[32,32]{0,1:T(8,128)S(1)}, u32[]{:S(2)}, u32[]{:S(2)}) %collective-permute-start.1) | collective-permute-done | bytes 4128 | tf_op jit(solution)/shard_map/ppermute | solution.py:19
  133.3 0.8 scatter_custom_fusion.1
  134.2 0.7 copy.33
  (16 shorter events, 0.1 us)
Async XLA Ops:
  6.5 1.1 copy-start
  6.5 22.5 %all-gather.3.cloned.1.call-start = ((), (), s32[]{:S(2)}) async-start(), calls=%async_computation.1 | async-start | bytes 7077888 | tf_op jit(solution)/shard_map/all_gather | solution.py:39
  13.0 0.7 copy-start.3
  50.1 8.4 %copy-start.2 = (bf16[1,16,32,108]{3,2,1,0:T(8,128)(2,1)S(1)}, bf16[1,16,32,108]{3,2,1,0:T(8,128)(2,1)}, u32[]{:S(2)}) copy-start(bf16[1,16,32,108]{3,2,1,0:T(8,128)(2,1)} %param.9) | copy-start | bytes 331780
  51.4 10.0 %copy-start.4 = (s32[3,1,16,32]{3,2,1,0:T(8,128)S(1)}, s32[3,1,16,32]{3,2,1,0:T(8,128)}, u32[]{:S(2)}) copy-start(s32[3,1,16,32]{3,2,1,0:T(8,128)} %param.10) | copy-start | bytes 18436
  51.4 10.1 %copy-start.5 = (s32[1,2,32]{2,1,0:T(2,128)S(1)}, s32[1,2,32]{2,1,0:T(2,128)}, u32[]{:S(2)}) copy-start(s32[1,2,32]{2,1,0:T(2,128)} %param.11) | copy-start | bytes 772
  51.4 33.9 %all-to-all-start = ((bf16[16,32,1152]{2,1,0:T(8,128)(2,1)}), bf16[16,32,1152]{2,1,0:T(8,128)(2,1)S(1)}, u32[]{:S(2)}, u32[]{:S(2)}) async-start(bf16[16,32,1152]{2,1,0:T(8,128)(2,1)} %broadcast_select_fusion), calls=%async_computation | async-start | bytes 2359296 | tf_op jit(solution)/shard_map/all_to_all | solution.py:50
  88.6 19.7 %copy-start.1 = (bf16[16,32,3,12,3,1]{3,2,4,5,1,0:T(4,128)(2,1)S(1)}, bf16[16,32,3,12,3,1]{3,2,4,5,1,0:T(4,128)(2,1)}, u32[]{:S(2)}) copy-start(bf16[16,32,3,12,3,1]{3,2,4,5,1,0:T(4,128)(2,1)} %copy.36) | copy-start | bytes 331780
  119.9 7.9 %collective-permute-start = (f32[32,32]{0,1:T(8,128)S(1)}, f32[32,32]{0,1:T(8,128)S(1)}, u32[]{:S(2)}, u32[]{:S(2)}) collective-permute-start(f32[32,32]{0,1:T(8,128)S(1)} %bitcast.63), channel_id=1, source_target_pairs={{0,2},{2,4},{4,6},{6,8},{8,10},{10,12},{12,14},{14,16},{16,18},{18... | collective-permute-start | bytes 12296 | tf_op jit(solution)/shard_map/ppermute | solution.py:18
  125.9 7.4 %collective-permute-start.1 = (f32[32,32]{0,1:T(8,128)S(1)}, f32[32,32]{0,1:T(8,128)S(1)}, u32[]{:S(2)}, u32[]{:S(2)}) collective-permute-start(f32[32,32]{0,1:T(8,128)S(1)} %bitcast.62), channel_id=1, source_target_pairs={{2,0},{4,2},{6,4},{8,6},{10,8},{12,10},{14,12},{16,14},{18,16},{20... | collective-permute-start | bytes 12296 | tf_op jit(solution)/shard_map/ppermute | solution.py:19
Sparse Core Ops, SparseCore 0:
  13.2 15.8 all-gather.2
